TPU v7x, 512 devices: a whole 4x4x16 slice. The times are simulated.
512 devices in a mesh: gx: 4 (over z_hi), gy: 16 (over y, x), gz: 8 (over z_lo, core).
Axes of the slice: x: 4, y: 4, z: 16 (z_hi: 4, z_lo: 4; z = z_hi * 4 + z_lo), core: 2. Of those that a mesh axis runs over, the one named last changes fastest.
Arguments:
- features: float32 [4, 32, 8, 128, 256], P('gx', 'gy', 'gz'), may hold values from -82 to 82
- occupancy: int32 [4, 32, 8], P('gx', 'gy', 'gz'), may hold values from 1 to 128, as said below
- dest_bin: int32 [4, 32, 8], P('gx', 'gy', 'gz'), may hold values from 0 to 1023, as said below
- query_weight: bfloat16 [256, 256], replicated, may hold values from -0.375 to 0.375
- key_weight: bfloat16 [256, 256], replicated, may hold values from -0.375 to 0.375
- value_weight: bfloat16 [256, 256], replicated, may hold values from -0.375 to 0.375
- out_weight: bfloat16 [256, 256], replicated, may hold values from -0.375 to 0.375
- up_weight: bfloat16 [256, 1024], replicated, may hold values from -0.375 to 0.375
- down_weight: bfloat16 [1024, 256], replicated, may hold values from -0.1875 to 0.1875
- attention_gain: float32 [256], replicated, may hold values from 0.25 to 1.75
- feed_gain: float32 [256], replicated, may hold values from 0.25 to 1.75
Outputs:
- particles: float32 [4, 32, 8, 128, 256], P('gx', 'gy', 'gz')
Inputs may be any that keep to these rules, and one draw needn't show every extreme that they name: `occupancy`: some bin holds 128 live particles. `dest_bin`: A permutation of the bins; every block stays on a device with the same gx and gy index, and each device sends at most 1 block to any one device, a bound that some pair of devices reaches.
All inputs are finite; a program needn't handle non-finite values.
Results may differ from a plain program's by a relative error of at most 0.0065.
The roundings to bfloat16 on the way count: a program that leaves them out, or rounds other values in their place, can miss the bound.
Values may be sent and summed in bfloat16 or wider, within the bound.
A program may use at most 64 MiB of HBM per device.

v0:
```python
import jax
import jax.numpy as jnp
from jax import lax
from jax.sharding import PartitionSpec as P

HEADS = 8
LAYERS = 2


EPSILON = 1e-05


def padded_2(cells, sides, width):
    for axis, dim in sides:
        count = lax.axis_size(axis)
        ends = count - 1
        head = lax.slice_in_dim(cells, 0, width, axis=dim)
        tail = lax.slice_in_dim(cells, cells.shape[dim] - width, cells.shape[dim], axis=dim)
        cells = jnp.concatenate(
            [
                lax.ppermute(tail, axis, [(i, (i + 1) % count) for i in range(ends)]),
                cells,
                lax.ppermute(head, axis, [((i + 1) % count, i) for i in range(ends)]),
            ],
            axis=dim,
        )
    return cells


def layer_norm(values, gain):
    centre = values - jnp.mean(values, axis=-1, keepdims=True)
    spread = jnp.mean(centre * centre, axis=-1, keepdims=True)
    return centre * lax.rsqrt(spread + EPSILON) * gain


def neighbours(padded):
    parts = [
        padded[1:-1, 1:-1, 1:-1],
        padded[:-2, 1:-1, 1:-1],
        padded[2:, 1:-1, 1:-1],
        padded[1:-1, :-2, 1:-1],
        padded[1:-1, 2:, 1:-1],
        padded[1:-1, 1:-1, :-2],
        padded[1:-1, 1:-1, 2:],
    ]
    return jnp.stack(parts, axis=3)


def attend(query, keys, values, mask, heads):
    batch, slots, width = query.shape
    head_size = width // heads
    total_keys = keys.shape[1]
    query_heads = query.reshape(batch, slots, heads, head_size)
    key_heads = keys.reshape(batch, total_keys, heads, head_size)
    value_heads = values.reshape(batch, total_keys, heads, head_size)
    scores = jnp.einsum(
        "bqhd,bkhd->bhqk", query_heads, key_heads, preferred_element_type=jnp.float32
    ) * head_size ** (-0.5)
    valid = mask[:, None, None, :]
    scores = jnp.where(valid, scores, -1e30)
    peak = jnp.max(scores, axis=-1, keepdims=True)
    weights = jnp.where(valid, jnp.exp(scores - peak), 0.0)
    weights = (weights / jnp.sum(weights, axis=-1, keepdims=True)).astype(jnp.bfloat16)
    mixed = jnp.einsum("bhqk,bkhd->bqhd", weights, value_heads, preferred_element_type=jnp.float32)
    return mixed.astype(jnp.bfloat16).reshape(batch, slots, width)


def update(rows, attended, occupied, out_weight, up_weight, down_weight, attention_gain, feed_gain):
    batch, slots, width = rows.shape
    mixed = jnp.dot(attended.reshape(-1, width), out_weight, preferred_element_type=jnp.float32)
    hidden = layer_norm(rows.reshape(-1, width) + mixed, attention_gain)
    inner = jax.nn.gelu(
        jnp.dot(hidden.astype(jnp.bfloat16), up_weight, preferred_element_type=jnp.float32)
    ).astype(jnp.bfloat16)
    grown = jnp.dot(inner, down_weight, preferred_element_type=jnp.float32)
    result = layer_norm(hidden + grown, feed_gain).reshape(batch, slots, width)
    live = jnp.arange(slots, dtype=jnp.int32)[None, :, None] < occupied[:, None, None]
    return jnp.where(live, result, 0.0)


def project_pair(flat, key_weight, value_weight):
    return jnp.concatenate(
        [
            jnp.dot(flat, key_weight, preferred_element_type=jnp.float32),
            jnp.dot(flat, value_weight, preferred_element_type=jnp.float32),
        ],
        axis=1,
    ).astype(jnp.bfloat16)


def local_layer(
    state,
    counts,
    query_weight,
    key_weight,
    value_weight,
    out_weight,
    up_weight,
    down_weight,
    attention_gain,
    feed_gain,
):
    bins_x, bins_y, bins_z, slots, width = state.shape
    total = bins_x * bins_y * bins_z
    rounded = state.astype(jnp.bfloat16)
    flat = rounded.reshape(-1, width)
    query = (
        jnp.dot(flat, query_weight, preferred_element_type=jnp.float32)
        .astype(jnp.bfloat16)
        .reshape(total, slots, width)
    )
    keyval = project_pair(flat, key_weight, value_weight).reshape(
        bins_x, bins_y, bins_z, slots, 2 * width
    )
    padded, padded_counts = (
        padded_2(keyval, (("gx", 0), ("gy", 1), ("gz", 2)), 1),
        padded_2(counts, (("gx", 0), ("gy", 1), ("gz", 2)), 1),
    )
    keys = neighbours(padded).reshape(total, 7 * slots, 2 * width)
    near = neighbours(padded_counts).reshape(total, 7)
    mask = (jnp.arange(slots, dtype=jnp.int32)[None, None, :] < near[:, :, None]).reshape(
        total, 7 * slots
    )
    groups = max(1, width // 128)
    columns = width // groups
    pieces = []
    for group in range(groups):
        start = group * columns
        pieces.append(
            attend(
                query[..., start : start + columns],
                keys[..., start : start + columns],
                keys[..., width + start : width + start + columns],
                mask,
                HEADS // groups,
            )
        )
    attended = jnp.concatenate(pieces, axis=-1)
    result = update(
        state.reshape(total, slots, width),
        attended,
        counts.reshape(-1),
        out_weight,
        up_weight,
        down_weight,
        attention_gain,
        feed_gain,
    )
    return result.reshape(state.shape)


def relocate(state, counts, dest_bin):
    bins_x, bins_y, bins_z, slots, width = state.shape
    total = bins_x * bins_y * bins_z
    depth = lax.axis_size("gz")
    span_y = bins_y * lax.axis_size("gy")
    span_z = bins_z * depth
    targets = dest_bin.reshape(-1)
    target_z = targets % span_z
    target_y = targets // span_z % span_y
    target_x = targets // (span_z * span_y)
    peer = target_z // bins_z
    local = (target_x % bins_x * bins_y + target_y % bins_y) * bins_z + target_z % bins_z
    order = jnp.arange(total, dtype=jnp.int32)
    earlier = (peer[None, :] == peer[:, None]) & (order[None, :] < order[:, None])
    slot = jnp.sum(earlier.astype(jnp.int32), axis=1)
    capacity = (total + depth - 1) // depth
    outgoing = (
        jnp.zeros((depth, capacity, slots, width), jnp.float32)
        .at[peer, slot]
        .set(state.reshape(total, slots, width))
    )
    outgoing_counts = jnp.zeros((depth, capacity), jnp.int32).at[peer, slot].set(counts.reshape(-1))
    outgoing_places = jnp.full((depth, capacity), total, jnp.int32).at[peer, slot].set(local)
    arrived, arrived_counts, arrived_places = (
        lax.all_to_all(
            outgoing.astype(jnp.bfloat16), "gz", split_axis=0, concat_axis=0, tiled=True
        ).astype(outgoing.dtype),
        lax.all_to_all(outgoing_counts, "gz", split_axis=0, concat_axis=0, tiled=True),
        lax.all_to_all(outgoing_places, "gz", split_axis=0, concat_axis=0, tiled=True),
    )
    places = arrived_places.reshape(-1)
    moved = (
        jnp.zeros((total, slots, width), jnp.float32)
        .at[places]
        .set(arrived.reshape(-1, slots, width), mode="drop")
    )
    moved_counts = (
        jnp.zeros((total,), jnp.int32).at[places].set(arrived_counts.reshape(-1), mode="drop")
    )
    return (moved.reshape(state.shape), moved_counts.reshape(counts.shape))


def shards(
    features,
    occupancy,
    dest_bin,
    query_weight,
    key_weight,
    value_weight,
    out_weight,
    up_weight,
    down_weight,
    attention_gain,
    feed_gain,
):
    state, counts = (features, occupancy)
    for layer in range(LAYERS):
        state = local_layer(
            state,
            counts,
            query_weight,
            key_weight,
            value_weight,
            out_weight,
            up_weight,
            down_weight,
            attention_gain,
            feed_gain,
        )
        if layer + 1 < LAYERS:
            state, counts = relocate(state, counts, dest_bin)
    return state


def solution(mesh):
    placed = (
        P("gx", "gy", "gz", None, None),
        P("gx", "gy", "gz"),
        P("gx", "gy", "gz"),
        P(),
        P(),
        P(),
        P(),
        P(),
        P(),
        P(),
        P(),
    )
    return jax.shard_map(
        shards,
        mesh=mesh,
        in_specs=placed,
        out_specs=P("gx", "gy", "gz", None, None),
        check_vma=False,
    )
```

profile of v0, /device:TPU:23, one launch (start us, length us, event | category | flops | bytes accessed | tf_op | source)
XLA Modules:
  0.0 276.6 jit_solution(416495408467343556)
XLA Ops:
  0.0 1.1 convert_element_type.99
  1.1 1.1 convolution_convert_fusion.4
  2.2 1.1 convolution_convert_fusion.5
  3.3 8.8 %collective-permute-start = (bf16[1,2,1,128,512]{4,3,1,2,0:T(8,128)(2,1)S(1)}, bf16[1,2,1,128,512]{4,3,1,2,0:T(8,128)(2,1)S(1)}, u32[]{:S(2)}, u32[]{:S(2)}) collective-permute-start(bf16[1,2,1,128,512]{4,3,1,2,0:T(8,128)(2,1)S(1)} %pad_maximum_fusion.20), channel_id=1, source_target_pairs={{0,128},{128,256},{256,384},{1,129},{129,257},{257,385},{2,130},{1... | collective-permute-start | bytes 786440 | tf_op jit(solution)/shard_map/ppermute | solution.py:21
  12.1 1.3 collective-permute-start.1
  13.4 9.4 %collective-permute-start.6 = (s32[1,2,1]{1,2,0:T(1,128)}, s32[1,2,1]{1,2,0:T(1,128)S(1)}, u32[]{:S(2)}, u32[]{:S(2)}) collective-permute-start(s32[1,2,1]{1,2,0:T(1,128)} %param.12), channel_id=1, source_target_pairs={{0,128},{128,256},{256,384},{1,129},{129,257},{257,385},{2,130},{1... | collective-permute-start | bytes 32 | tf_op jit(solution)/shard_map/ppermute | solution.py:21
  22.9 1.3 collective-permute-start.7
  27.0 5.9 %all-to-all-start = ((s32[8,1,1]{2,1,0:T(1,128)}), s32[8,1,1]{2,1,0:T(1,128)S(1)}, u32[]{:S(2)}, u32[]{:S(2)}) async-start(s32[8,1,1]{2,1,0:T(1,128)} %copy.148), calls=%async_computation | async-start | bytes 8192 | tf_op jit(solution)/shard_map/all_to_all | solution.py:180
  32.9 1.3 iota_compare_fusion
  38.1 6.0 %collective-permute-done.7 = s32[1,2,1]{1,2,0:T(1,128)S(1)} collective-permute-done((s32[1,2,1]{1,2,0:T(1,128)}, s32[1,2,1]{1,2,0:T(1,128)S(1)}, u32[]{:S(2)}, u32[]{:S(2)}) %collective-permute-start.7) | collective-permute-done | bytes 40 | tf_op jit(solution)/shard_map/ppermute | solution.py:23
  44.3 2.4 collective-permute-start.9
  46.8 4.9 %collective-permute-start.8 = (s32[3,1,1]{1,2,0:T(1,128)S(1)}, s32[3,1,1]{1,2,0:T(1,128)S(1)}, u32[]{:S(2)}, u32[]{:S(2)}) collective-permute-start(s32[3,1,1]{1,2,0:T(1,128)S(1)} %get-tuple-element.30), channel_id=1, source_target_pairs={{0,8},{8,16},{16,24},{24,32},{32,40},{40,48},{48,56},{56,64},{64,7... | collective-permute-start | bytes 44 | tf_op jit(solution)/shard_map/ppermute | solution.py:21
  52.5 1.9 collective-permute-start.10
  54.4 3.5 %collective-permute-start.11 = (s32[3,4,1]{1,2,0:T(1,128)S(1)}, s32[3,4,1]{1,2,0:T(1,128)S(1)}, u32[]{:S(2)}, u32[]{:S(2)}) collective-permute-start(s32[3,4,1]{1,2,0:T(1,128)S(1)} %pad_add_fusion), channel_id=1, source_target_pairs={{1,0},{2,1},{3,2},{4,3},{5,4},{6,5},{7,6},{9,8},{10,9},{11,10},{12... | collective-permute-start | bytes 152 | tf_op jit(solution)/shard_map/ppermute | solution.py:23
  58.3 1.1 collective-permute-done.11
  59.6 3.2 %all-to-all-start.1 = ((s32[8,1,1]{2,1,0:T(1,128)}), s32[8,1,1]{2,1,0:T(1,128)S(1)}, u32[]{:S(2)}, u32[]{:S(2)}) async-start(s32[8,1,1]{2,1,0:T(1,128)} %copy.149), calls=%async_computation.1 | async-start | bytes 8192 | tf_op jit(solution)/shard_map/all_to_all | solution.py:179
  63.7 3.7 %all-to-all-done.1 = s32[8,1,1]{2,1,0:T(1,128)S(1)} async-done(((s32[8,1,1]{2,1,0:T(1,128)}), s32[8,1,1]{2,1,0:T(1,128)S(1)}, u32[]{:S(2)}, u32[]{:S(2)}) %all-to-all-start.1) | async-done | bytes 64 | tf_op jit(solution)/shard_map/all_to_all | solution.py:179
  68.3 7.3 %collective-permute-start.18 = (s32[1,2,1]{1,2,0:T(1,128)S(1)}, s32[1,2,1]{1,2,0:T(1,128)S(1)}, u32[]{:S(2)}, u32[]{:S(2)}) collective-permute-start(s32[1,2,1]{1,2,0:T(1,128)S(1)} %bitcast.308), channel_id=1, source_target_pairs={{0,128},{128,256},{256,384},{1,129},{129,257},{257,385},{2,130},{1... | collective-permute-start | bytes 32 | tf_op jit(solution)/shard_map/ppermute | solution.py:21
  75.6 1.3 collective-permute-start.19
  78.2 5.5 %collective-permute-done.19 = s32[1,2,1]{1,2,0:T(1,128)S(1)} collective-permute-done((s32[1,2,1]{1,2,0:T(1,128)S(1)}, s32[1,2,1]{1,2,0:T(1,128)S(1)}, u32[]{:S(2)}, u32[]{:S(2)}) %collective-permute-start.19) | collective-permute-done | bytes 40 | tf_op jit(solution)/shard_map/ppermute | solution.py:23
  84.5 0.9 fusion.147
  85.5 6.0 %collective-permute-start.2 = (bf16[3,1,1,128,512]{4,3,1,2,0:T(8,128)(2,1)}, bf16[3,1,1,128,512]{4,3,1,2,0:T(8,128)(2,1)}, u32[]{:S(2)}, u32[]{:S(2)}) collective-permute-start(bf16[3,1,1,128,512]{4,3,1,2,0:T(8,128)(2,1)} %get-tuple-element.16), channel_id=1, source_target_pairs={{0,8},{8,16},{16,24},{24,32},{32,40},{40,48},{48,56},{56,64},{64,7... | collective-permute-start | bytes 1179656 | tf_op jit(solution)/shard_map/ppermute | solution.py:21
  91.5 1.9 collective-permute-start.3
  93.5 1.9 collective-permute-start.21
  95.4 5.5 %collective-permute-start.20 = (s32[3,1,1]{1,2,0:T(1,128)S(1)}, s32[3,1,1]{1,2,0:T(1,128)S(1)}, u32[]{:S(2)}, u32[]{:S(2)}) collective-permute-start(s32[3,1,1]{1,2,0:T(1,128)S(1)} %get-tuple-element.26), channel_id=1, source_target_pairs={{0,8},{8,16},{16,24},{24,32},{32,40},{40,48},{48,56},{56,64},{64,7... | collective-permute-start | bytes 44 | tf_op jit(solution)/shard_map/ppermute | solution.py:21
  100.9 3.0 %collective-permute-done.21 = s32[3,1,1]{1,2,0:T(1,128)S(1)} collective-permute-done((s32[3,1,1]{1,2,0:T(1,128)S(1)}, s32[3,1,1]{1,2,0:T(1,128)S(1)}, u32[]{:S(2)}, u32[]{:S(2)}) %collective-permute-start.21) | collective-permute-done | bytes 44 | tf_op jit(solution)/shard_map/ppermute | solution.py:23
  104.6 5.4 %collective-permute-start.22 = (s32[3,4,1]{1,2,0:T(1,128)}, s32[3,4,1]{1,2,0:T(1,128)}, u32[]{:S(2)}, u32[]{:S(2)}) collective-permute-start(s32[3,4,1]{1,2,0:T(1,128)} %pad_add_fusion.2), channel_id=1, source_target_pairs={{0,1},{1,2},{2,3},{3,4},{4,5},{5,6},{6,7},{8,9},{9,10},{10,11},{11... | collective-permute-start | bytes 152 | tf_op jit(solution)/shard_map/ppermute | solution.py:21
  110.0 1.9 collective-permute-start.23
  113.4 1.3 copy.185
  114.7 2.3 pad_maximum_fusion
  117.0 3.6 %collective-permute-start.4 = (bf16[3,4,1,128,512]{4,3,1,2,0:T(8,128)(2,1)}, bf16[3,4,1,128,512]{4,3,1,2,0:T(8,128)(2,1)}, u32[]{:S(2)}, u32[]{:S(2)}) collective-permute-start(bf16[3,4,1,128,512]{4,3,1,2,0:T(8,128)(2,1)} %pad_maximum_fusion), channel_id=1, source_target_pairs={{0,1},{1,2},{2,3},{3,4},{4,5},{5,6},{6,7},{8,9},{9,10},{10,11},{11... | collective-permute-start | bytes 4718600 | tf_op jit(solution)/shard_map/ppermute | solution.py:21
  122.0 1.9 collective-permute-start.5
  127.9 10.4 %collective-permute-done.4 = bf16[3,4,1,128,512]{4,3,1,2,0:T(8,128)(2,1)} collective-permute-done((bf16[3,4,1,128,512]{4,3,1,2,0:T(8,128)(2,1)}, bf16[3,4,1,128,512]{4,3,1,2,0:T(8,128)(2,1)}, u32[]{:S(2)}, u32[]{:S(2)}) %collective-permute-start.4) | collective-permute-done | bytes 1572896 | tf_op jit(solution)/shard_map/ppermute | solution.py:21
  138.3 1.0 fusion.73
  139.3 4.8 %collective-permute-done.5 = bf16[3,4,1,128,512]{4,3,1,2,0:T(8,128)(2,1)} collective-permute-done((bf16[3,4,1,128,512]{4,3,1,2,0:T(8,128)(2,1)}, bf16[3,4,1,128,512]{4,3,1,2,0:T(8,128)(2,1)}, u32[]{:S(2)}, u32[]{:S(2)}) %collective-permute-start.5) | collective-permute-done | bytes 1572896 | tf_op jit(solution)/shard_map/ppermute | solution.py:23
  144.1 1.0 fusion.72
  145.0 1.3 fusion.145
  146.3 1.3 copy.168
  147.6 1.3 copy.170
  148.9 3.2 %fusion.152 = (f32[2,4,128]{2,1,0:T(4,128)S(1)}, f32[2,4,128,896]{3,2,1,0:T(8,128)}) fusion(pred[2,896]{1,0:T(4,128)(4,1)S(1)} %get-tuple-element.22, bf16[2,128,4,32]{1,3,2,0:T(8,128)(2,1)S(1)} %bitcast.305, bf16[2,896,4,32]{1,3,2,0:T(8,128)(2,1)S(1)} %bitcast.295), kind=kOutput, calls=%fused_computation.260 | convolution fusion | flops 63308672 | bytes 4200192 | tf_op jit(solution)/shard_map/sub | solution.py:62
  152.1 2.9 %fusion.29 = bf16[2,128,4,32]{1,3,2,0:T(8,128)(2,1)S(1)} fusion(bf16[2,896,4,32]{1,3,2,0:T(8,128)(2,1)S(1)} %bitcast.291, f32[2,4,128,896]{3,2,1,0:T(8,128)} %get-tuple-element.34, f32[2,4,128]{2,1,0:T(4,128)S(1)} %get-tuple-element.33), kind=kOutput, calls=%fused_computation.60 | convolution fusion | flops 60588032 | bytes 4198400 | tf_op jit(solution)/shard_map/bhqk,bkhd->bqhd/dot_general | solution.py:64
  155.9 3.2 %fusion.153 = (f32[2,4,128]{2,1,0:T(4,128)S(1)}, f32[2,4,128,896]{3,2,1,0:T(8,128)}) fusion(pred[2,896]{1,0:T(4,128)(4,1)S(1)} %get-tuple-element.22, bf16[2,128,4,32]{1,3,2,0:T(8,128)(2,1)S(1)} %bitcast.304, bf16[2,896,4,32]{1,3,2,0:T(8,128)(2,1)S(1)} %bitcast.292), kind=kOutput, calls=%fused_computation.261 | convolution fusion | flops 63308672 | bytes 4200192 | tf_op jit(solution)/shard_map/sub | solution.py:62
  159.1 2.9 %fusion.28 = bf16[2,128,4,32]{1,3,2,0:T(8,128)(2,1)S(1)} fusion(bf16[2,896,4,32]{1,3,2,0:T(8,128)(2,1)S(1)} %bitcast.288, f32[2,4,128,896]{3,2,1,0:T(8,128)} %get-tuple-element.36, f32[2,4,128]{2,1,0:T(4,128)S(1)} %get-tuple-element.35), kind=kOutput, calls=%fused_computation.59 | convolution fusion | flops 60588032 | bytes 4198400 | tf_op jit(solution)/shard_map/bhqk,bkhd->bqhd/dot_general | solution.py:64
  164.8 16.0 %all_to_all.26 = bf16[8,1,128,256]{3,2,1,0:T(8,128)(2,1)S(1)} all-to-all(bf16[8,1,128,256]{3,2,1,0:T(8,128)(2,1)S(1)} %convert_bitcast_fusion), channel_id=1, replica_groups=mesh['gx'=4,'gy'=16,'gz'=8] {'gz'}, dimensions={0} | all-to-all | bytes 1048576 | tf_op jit(solution)/shard_map/all_to_all | solution.py:176
  182.3 4.6 %collective-permute-start.12 = (bf16[1,2,1,128,512]{4,3,1,2,0:T(8,128)(2,1)S(1)}, bf16[1,2,1,128,512]{4,3,1,2,0:T(8,128)(2,1)S(1)}, u32[]{:S(2)}, u32[]{:S(2)}) collective-permute-start(bf16[1,2,1,128,512]{4,3,1,2,0:T(8,128)(2,1)S(1)} %pad_maximum_fusion.21), channel_id=1, source_target_pairs={{0,128},{128,256},{256,384},{1,129},{129,257},{257,385},{2,130},{1... | collective-permute-start | bytes 786440 | tf_op jit(solution)/shard_map/ppermute | solution.py:21
  186.9 1.3 collective-permute-start.13
  188.2 3.5 %collective-permute-done.12 = bf16[1,2,1,128,512]{4,3,1,2,0:T(8,128)(2,1)S(1)} collective-permute-done((bf16[1,2,1,128,512]{4,3,1,2,0:T(8,128)(2,1)S(1)}, bf16[1,2,1,128,512]{4,3,1,2,0:T(8,128)(2,1)S(1)}, u32[]{:S(2)}, u32[]{:S(2)}) %collective-permute-start.12) | collective-permute-done | bytes 262176 | tf_op jit(solution)/shard_map/ppermute | solution.py:21
  191.7 25.1 %collective-permute-done.13 = bf16[1,2,1,128,512]{4,3,1,2,0:T(8,128)(2,1)S(1)} collective-permute-done((bf16[1,2,1,128,512]{4,3,1,2,0:T(8,128)(2,1)S(1)}, bf16[1,2,1,128,512]{4,3,1,2,0:T(8,128)(2,1)S(1)}, u32[]{:S(2)}, u32[]{:S(2)}) %collective-permute-start.13) | collective-permute-done | bytes 262176 | tf_op jit(solution)/shard_map/ppermute | solution.py:23
  217.0 4.0 %collective-permute-start.14 = (bf16[3,1,1,128,512]{4,3,1,2,0:T(8,128)(2,1)S(1)}, bf16[3,1,1,128,512]{4,3,1,2,0:T(8,128)(2,1)S(1)}, u32[]{:S(2)}, u32[]{:S(2)}) collective-permute-start(bf16[3,1,1,128,512]{4,3,1,2,0:T(8,128)(2,1)S(1)} %get-tuple-element.14), channel_id=1, source_target_pairs={{0,8},{8,16},{16,24},{24,32},{32,40},{40,48},{48,56},{56,64},{64,7... | collective-permute-start | bytes 1179656 | tf_op jit(solution)/shard_map/ppermute | solution.py:21
  221.0 1.9 collective-permute-start.15
  222.9 6.3 %collective-permute-done.14 = bf16[3,1,1,128,512]{4,3,1,2,0:T(8,128)(2,1)S(1)} collective-permute-done((bf16[3,1,1,128,512]{4,3,1,2,0:T(8,128)(2,1)S(1)}, bf16[3,1,1,128,512]{4,3,1,2,0:T(8,128)(2,1)S(1)}, u32[]{:S(2)}, u32[]{:S(2)}) %collective-permute-start.14) | collective-permute-done | bytes 393248 | tf_op jit(solution)/shard_map/ppermute | solution.py:21
  229.2 5.6 %collective-permute-done.15 = bf16[3,1,1,128,512]{4,3,1,2,0:T(8,128)(2,1)S(1)} collective-permute-done((bf16[3,1,1,128,512]{4,3,1,2,0:T(8,128)(2,1)S(1)}, bf16[3,1,1,128,512]{4,3,1,2,0:T(8,128)(2,1)S(1)}, u32[]{:S(2)}, u32[]{:S(2)}) %collective-permute-start.15) | collective-permute-done | bytes 393248 | tf_op jit(solution)/shard_map/ppermute | solution.py:23
  235.0 1.9 collective-permute-start.16
  236.9 4.3 %collective-permute-start.17 = (bf16[3,4,1,128,512]{4,3,1,2,0:T(8,128)(2,1)S(1)}, bf16[3,4,1,128,512]{4,3,1,2,0:T(8,128)(2,1)}, u32[]{:S(2)}, u32[]{:S(2)}) collective-permute-start(bf16[3,4,1,128,512]{4,3,1,2,0:T(8,128)(2,1)S(1)} %pad_maximum_fusion.1), channel_id=1, source_target_pairs={{1,0},{2,1},{3,2},{4,3},{5,4},{6,5},{7,6},{9,8},{10,9},{11,10},{12... | collective-permute-start | bytes 4718600 | tf_op jit(solution)/shard_map/ppermute | solution.py:23
  242.1 1.6 copy.192
  243.7 1.6 copy.188
  246.3 8.0 %collective-permute-done.16 = bf16[3,4,1,128,512]{4,3,1,2,0:T(8,128)(2,1)} collective-permute-done((bf16[3,4,1,128,512]{4,3,1,2,0:T(8,128)(2,1)S(1)}, bf16[3,4,1,128,512]{4,3,1,2,0:T(8,128)(2,1)}, u32[]{:S(2)}, u32[]{:S(2)}) %collective-permute-start.16) | collective-permute-done | bytes 1572896 | tf_op jit(solution)/shard_map/ppermute | solution.py:21
  254.3 1.0 fusion.67
  255.2 3.5 %collective-permute-done.17 = bf16[3,4,1,128,512]{4,3,1,2,0:T(8,128)(2,1)} collective-permute-done((bf16[3,4,1,128,512]{4,3,1,2,0:T(8,128)(2,1)S(1)}, bf16[3,4,1,128,512]{4,3,1,2,0:T(8,128)(2,1)}, u32[]{:S(2)}, u32[]{:S(2)}) %collective-permute-start.17) | collective-permute-done | bytes 1572896 | tf_op jit(solution)/shard_map/ppermute | solution.py:23
  258.8 1.0 fusion.66
  260.9 3.2 %fusion.158 = (f32[2,4,128]{2,1,0:T(4,128)S(1)}, f32[2,4,128,896]{3,2,1,0:T(8,128)}) fusion(pred[2,896]{1,0:T(4,128)(4,1)S(1)} %get-tuple-element.21, bf16[2,128,4,32]{1,3,2,0:T(8,128)(2,1)S(1)} %bitcast.307, bf16[2,896,4,32]{1,3,2,0:T(8,128)(2,1)S(1)} %bitcast.293), kind=kOutput, calls=%fused_computation.264 | convolution fusion | flops 63308672 | bytes 4200192 | tf_op jit(solution)/shard_map/sub | solution.py:62
  264.2 2.8 %fusion.31 = bf16[2,128,4,32]{1,3,2,0:T(8,128)(2,1)S(1)} fusion(bf16[2,896,4,32]{1,3,2,0:T(8,128)(2,1)S(1)} %bitcast.290, f32[2,4,128,896]{3,2,1,0:T(8,128)} %get-tuple-element.42, f32[2,4,128]{2,1,0:T(4,128)S(1)} %get-tuple-element.41), kind=kOutput, calls=%fused_computation.62 | convolution fusion | flops 60588032 | bytes 4198400 | tf_op jit(solution)/shard_map/bhqk,bkhd->bqhd/dot_general | solution.py:64
  267.9 3.2 %fusion.159 = (f32[2,4,128]{2,1,0:T(4,128)S(1)}, f32[2,4,128,896]{3,2,1,0:T(8,128)}) fusion(pred[2,896]{1,0:T(4,128)(4,1)S(1)} %get-tuple-element.21, bf16[2,128,4,32]{1,3,2,0:T(8,128)(2,1)S(1)} %bitcast.306, bf16[2,896,4,32]{1,3,2,0:T(8,128)(2,1)S(1)} %bitcast.294), kind=kOutput, calls=%fused_computation.265 | convolution fusion | flops 63308672 | bytes 4200192 | tf_op jit(solution)/shard_map/sub | solution.py:62
  271.1 2.9 %fusion.30 = bf16[2,128,4,32]{1,3,2,0:T(8,128)(2,1)S(1)} fusion(bf16[2,896,4,32]{1,3,2,0:T(8,128)(2,1)S(1)} %bitcast.289, f32[2,4,128,896]{3,2,1,0:T(8,128)} %get-tuple-element.44, f32[2,4,128]{2,1,0:T(4,128)S(1)} %get-tuple-element.43), kind=kOutput, calls=%fused_computation.61 | convolution fusion | flops 60588032 | bytes 4198400 | tf_op jit(solution)/shard_map/bhqk,bkhd->bqhd/dot_general | solution.py:64
  (175 shorter events, 31.1 us)
Async XLA Ops:
  0.0 162.7 %copy-start = (bf16[1024,256]{1,0:T(8,128)(2,1)S(1)}, bf16[1024,256]{1,0:T(8,128)(2,1)}, u32[]{:S(2)}) copy-start(bf16[1024,256]{1,0:T(8,128)(2,1)} %param.19) | copy-start | bytes 1572868
  0.0 44.2 %copy-start.25 = (s32[1,2,1]{1,2,0:T(1,128)S(1)}, s32[1,2,1]{1,2,0:T(1,128)}, u32[]{:S(2)}) copy-start(s32[1,2,1]{1,2,0:T(1,128)} %param.12) | copy-start | bytes 28
  0.0 36.2 %copy-start.7 = (bf16[256,256]{1,0:T(8,128)(2,1)S(1)}, bf16[256,256]{1,0:T(8,128)(2,1)}, u32[]{:S(2)}) copy-start(bf16[256,256]{1,0:T(8,128)(2,1)} %param.14) | copy-start | bytes 393220
  3.3 81.1 %collective-permute-start = (bf16[1,2,1,128,512]{4,3,1,2,0:T(8,128)(2,1)S(1)}, bf16[1,2,1,128,512]{4,3,1,2,0:T(8,128)(2,1)S(1)}, u32[]{:S(2)}, u32[]{:S(2)}) collective-permute-start(bf16[1,2,1,128,512]{4,3,1,2,0:T(8,128)(2,1)S(1)} %pad_maximum_fusion.20), channel_id=1, source_target_pairs={{0,128},{128,256},{256,384},{1,129},{129,257},{257,385},{2,130},{1... | collective-permute-start | bytes 786440 | tf_op jit(solution)/shard_map/ppermute | solution.py:21
  12.1 72.3 %collective-permute-start.1 = (bf16[1,2,1,128,512]{4,3,1,2,0:T(8,128)(2,1)S(1)}, bf16[1,2,1,128,512]{4,3,1,2,0:T(8,128)(2,1)S(1)}, u32[]{:S(2)}, u32[]{:S(2)}) collective-permute-start(bf16[1,2,1,128,512]{4,3,1,2,0:T(8,128)(2,1)S(1)} %pad_maximum_fusion.20), channel_id=1, source_target_pairs={{128,0},{256,128},{384,256},{129,1},{257,129},{385,257},{130,2},{2... | collective-permute-start | bytes 786440 | tf_op jit(solution)/shard_map/ppermute | solution.py:23
  13.4 24.5 %collective-permute-start.6 = (s32[1,2,1]{1,2,0:T(1,128)}, s32[1,2,1]{1,2,0:T(1,128)S(1)}, u32[]{:S(2)}, u32[]{:S(2)}) collective-permute-start(s32[1,2,1]{1,2,0:T(1,128)} %param.12), channel_id=1, source_target_pairs={{0,128},{128,256},{256,384},{1,129},{129,257},{257,385},{2,130},{1... | collective-permute-start | bytes 32 | tf_op jit(solution)/shard_map/ppermute | solution.py:21
  22.9 21.2 %collective-permute-start.7 = (s32[1,2,1]{1,2,0:T(1,128)}, s32[1,2,1]{1,2,0:T(1,128)S(1)}, u32[]{:S(2)}, u32[]{:S(2)}) collective-permute-start(s32[1,2,1]{1,2,0:T(1,128)} %param.12), channel_id=1, source_target_pairs={{128,0},{256,128},{384,256},{129,1},{257,129},{385,257},{130,2},{2... | collective-permute-start | bytes 32 | tf_op jit(solution)/shard_map/ppermute | solution.py:23
  25.7 21.1 %copy-start.17 = (s32[2]{0:T(128)}, s32[2]{0:T(128)S(1)}, u32[]{:S(2)}) copy-start(s32[2]{0:T(128)S(1)} %fusion.119) | copy-start | bytes 28
  27.0 32.6 %all-to-all-start = ((s32[8,1,1]{2,1,0:T(1,128)}), s32[8,1,1]{2,1,0:T(1,128)S(1)}, u32[]{:S(2)}, u32[]{:S(2)}) async-start(s32[8,1,1]{2,1,0:T(1,128)} %copy.148), calls=%async_computation | async-start | bytes 8192 | tf_op jit(solution)/shard_map/all_to_all | solution.py:180
  44.3 7.4 %collective-permute-start.9 = (s32[3,1,1]{1,2,0:T(1,128)S(1)}, s32[3,1,1]{1,2,0:T(1,128)S(1)}, u32[]{:S(2)}, u32[]{:S(2)}) collective-permute-start(s32[3,1,1]{1,2,0:T(1,128)S(1)} %get-tuple-element.29), channel_id=1, source_target_pairs={{8,0},{16,8},{24,16},{32,24},{40,32},{48,40},{56,48},{64,56},{72,6... | collective-permute-start | bytes 44 | tf_op jit(solution)/shard_map/ppermute | solution.py:23
  46.8 5.7 %collective-permute-start.8 = (s32[3,1,1]{1,2,0:T(1,128)S(1)}, s32[3,1,1]{1,2,0:T(1,128)S(1)}, u32[]{:S(2)}, u32[]{:S(2)}) collective-permute-start(s32[3,1,1]{1,2,0:T(1,128)S(1)} %get-tuple-element.30), channel_id=1, source_target_pairs={{0,8},{8,16},{16,24},{24,32},{32,40},{40,48},{48,56},{56,64},{64,7... | collective-permute-start | bytes 44 | tf_op jit(solution)/shard_map/ppermute | solution.py:21
  52.5 5.7 %collective-permute-start.10 = (s32[3,4,1]{1,2,0:T(1,128)S(1)}, s32[3,4,1]{1,2,0:T(1,128)S(1)}, u32[]{:S(2)}, u32[]{:S(2)}) collective-permute-start(s32[3,4,1]{1,2,0:T(1,128)S(1)} %pad_add_fusion), channel_id=1, source_target_pairs={{0,1},{1,2},{2,3},{3,4},{4,5},{5,6},{6,7},{8,9},{9,10},{10,11},{11... | collective-permute-start | bytes 152 | tf_op jit(solution)/shard_map/ppermute | solution.py:21
  54.4 4.9 %collective-permute-start.11 = (s32[3,4,1]{1,2,0:T(1,128)S(1)}, s32[3,4,1]{1,2,0:T(1,128)S(1)}, u32[]{:S(2)}, u32[]{:S(2)}) collective-permute-start(s32[3,4,1]{1,2,0:T(1,128)S(1)} %pad_add_fusion), channel_id=1, source_target_pairs={{1,0},{2,1},{3,2},{4,3},{5,4},{6,5},{7,6},{9,8},{10,9},{11,10},{12... | collective-permute-start | bytes 152 | tf_op jit(solution)/shard_map/ppermute | solution.py:23
  59.6 7.8 %all-to-all-start.1 = ((s32[8,1,1]{2,1,0:T(1,128)}), s32[8,1,1]{2,1,0:T(1,128)S(1)}, u32[]{:S(2)}, u32[]{:S(2)}) async-start(s32[8,1,1]{2,1,0:T(1,128)} %copy.149), calls=%async_computation.1 | async-start | bytes 8192 | tf_op jit(solution)/shard_map/all_to_all | solution.py:179
  67.7 23.8 %copy-start.19 = (s32[8]{0:T(128)}, s32[8]{0:T(128)S(1)}, u32[]{:S(2)}) copy-start(s32[8]{0:T(128)S(1)} %fusion.114) | copy-start | bytes 100
  68.3 9.3 %collective-permute-start.18 = (s32[1,2,1]{1,2,0:T(1,128)S(1)}, s32[1,2,1]{1,2,0:T(1,128)S(1)}, u32[]{:S(2)}, u32[]{:S(2)}) collective-permute-start(s32[1,2,1]{1,2,0:T(1,128)S(1)} %bitcast.308), channel_id=1, source_target_pairs={{0,128},{128,256},{256,384},{1,129},{129,257},{257,385},{2,130},{1... | collective-permute-start | bytes 32 | tf_op jit(solution)/shard_map/ppermute | solution.py:21
  75.6 8.2 %collective-permute-start.19 = (s32[1,2,1]{1,2,0:T(1,128)S(1)}, s32[1,2,1]{1,2,0:T(1,128)S(1)}, u32[]{:S(2)}, u32[]{:S(2)}) collective-permute-start(s32[1,2,1]{1,2,0:T(1,128)S(1)} %bitcast.309), channel_id=1, source_target_pairs={{128,0},{256,128},{384,256},{129,1},{257,129},{385,257},{130,2},{2... | collective-permute-start | bytes 32 | tf_op jit(solution)/shard_map/ppermute | solution.py:23
  85.5 29.2 %collective-permute-start.2 = (bf16[3,1,1,128,512]{4,3,1,2,0:T(8,128)(2,1)}, bf16[3,1,1,128,512]{4,3,1,2,0:T(8,128)(2,1)}, u32[]{:S(2)}, u32[]{:S(2)}) collective-permute-start(bf16[3,1,1,128,512]{4,3,1,2,0:T(8,128)(2,1)} %get-tuple-element.16), channel_id=1, source_target_pairs={{0,8},{8,16},{16,24},{24,32},{32,40},{40,48},{48,56},{56,64},{64,7... | collective-permute-start | bytes 1179656 | tf_op jit(solution)/shard_map/ppermute | solution.py:21
  91.5 23.2 %collective-permute-start.3 = (bf16[3,1,1,128,512]{4,3,1,2,0:T(8,128)(2,1)}, bf16[3,1,1,128,512]{4,3,1,2,0:T(8,128)(2,1)S(1)}, u32[]{:S(2)}, u32[]{:S(2)}) collective-permute-start(bf16[3,1,1,128,512]{4,3,1,2,0:T(8,128)(2,1)} %get-tuple-element.15), channel_id=1, source_target_pairs={{8,0},{16,8},{24,16},{32,24},{40,32},{48,40},{56,48},{64,56},{72,6... | collective-permute-start | bytes 1179656 | tf_op jit(solution)/shard_map/ppermute | solution.py:23
  93.5 10.4 %collective-permute-start.21 = (s32[3,1,1]{1,2,0:T(1,128)S(1)}, s32[3,1,1]{1,2,0:T(1,128)S(1)}, u32[]{:S(2)}, u32[]{:S(2)}) collective-permute-start(s32[3,1,1]{1,2,0:T(1,128)S(1)} %get-tuple-element.25), channel_id=1, source_target_pairs={{8,0},{16,8},{24,16},{32,24},{40,32},{48,40},{56,48},{64,56},{72,6... | collective-permute-start | bytes 44 | tf_op jit(solution)/shard_map/ppermute | solution.py:23
  95.4 8.5 %collective-permute-start.20 = (s32[3,1,1]{1,2,0:T(1,128)S(1)}, s32[3,1,1]{1,2,0:T(1,128)S(1)}, u32[]{:S(2)}, u32[]{:S(2)}) collective-permute-start(s32[3,1,1]{1,2,0:T(1,128)S(1)} %get-tuple-element.26), channel_id=1, source_target_pairs={{0,8},{8,16},{16,24},{24,32},{32,40},{40,48},{48,56},{56,64},{64,7... | collective-permute-start | bytes 44 | tf_op jit(solution)/shard_map/ppermute | solution.py:21
  104.6 16.1 %collective-permute-start.22 = (s32[3,4,1]{1,2,0:T(1,128)}, s32[3,4,1]{1,2,0:T(1,128)}, u32[]{:S(2)}, u32[]{:S(2)}) collective-permute-start(s32[3,4,1]{1,2,0:T(1,128)} %pad_add_fusion.2), channel_id=1, source_target_pairs={{0,1},{1,2},{2,3},{3,4},{4,5},{5,6},{6,7},{8,9},{9,10},{10,11},{11... | collective-permute-start | bytes 152 | tf_op jit(solution)/shard_map/ppermute | solution.py:21
  110.0 13.9 %collective-permute-start.23 = (s32[3,4,1]{1,2,0:T(1,128)}, s32[3,4,1]{1,2,0:T(1,128)}, u32[]{:S(2)}, u32[]{:S(2)}) collective-permute-start(s32[3,4,1]{1,2,0:T(1,128)} %pad_add_fusion.2), channel_id=1, source_target_pairs={{1,0},{2,1},{3,2},{4,3},{5,4},{6,5},{7,6},{9,8},{10,9},{11,10},{12... | collective-permute-start | bytes 152 | tf_op jit(solution)/shard_map/ppermute | solution.py:23
  117.0 21.3 %collective-permute-start.4 = (bf16[3,4,1,128,512]{4,3,1,2,0:T(8,128)(2,1)}, bf16[3,4,1,128,512]{4,3,1,2,0:T(8,128)(2,1)}, u32[]{:S(2)}, u32[]{:S(2)}) collective-permute-start(bf16[3,4,1,128,512]{4,3,1,2,0:T(8,128)(2,1)} %pad_maximum_fusion), channel_id=1, source_target_pairs={{0,1},{1,2},{2,3},{3,4},{4,5},{5,6},{6,7},{8,9},{9,10},{10,11},{11... | collective-permute-start | bytes 4718600 | tf_op jit(solution)/shard_map/ppermute | solution.py:21
  122.0 22.0 %collective-permute-start.5 = (bf16[3,4,1,128,512]{4,3,1,2,0:T(8,128)(2,1)}, bf16[3,4,1,128,512]{4,3,1,2,0:T(8,128)(2,1)}, u32[]{:S(2)}, u32[]{:S(2)}) collective-permute-start(bf16[3,4,1,128,512]{4,3,1,2,0:T(8,128)(2,1)} %pad_maximum_fusion), channel_id=1, source_target_pairs={{1,0},{2,1},{3,2},{4,3},{5,4},{6,5},{7,6},{9,8},{10,9},{11,10},{12... | collective-permute-start | bytes 4718600 | tf_op jit(solution)/shard_map/ppermute | solution.py:23
  146.3 2.6 copy-start.12
  152.1 3.0 %copy-start.1 = (bf16[2,896,128]{2,1,0:T(8,128)(2,1)S(1)}, bf16[2,896,128]{2,1,0:T(8,128)(2,1)}, u32[]{:S(2)}) copy-start(bf16[2,896,128]{2,1,0:T(8,128)(2,1)} %get-tuple-element.12) | copy-start | bytes 1376260
  155.0 0.9 copy-start.11
  159.1 3.1 %copy-start.4 = (f32[1,2,1,128,256]{4,3,2,1,0:T(8,128)S(1)}, f32[1,2,1,128,256]{4,3,2,1,0:T(8,128)}, u32[]{:S(2)}) copy-start(f32[1,2,1,128,256]{4,3,2,1,0:T(8,128)} %param.11) | copy-start | bytes 786436
  159.1 3.1 %copy-start.9 = (bf16[256,256]{1,0:T(8,128)(2,1)S(1)}, bf16[256,256]{1,0:T(8,128)(2,1)}, u32[]{:S(2)}) copy-start(bf16[256,256]{1,0:T(8,128)(2,1)} %param.17) | copy-start | bytes 393220
  159.1 3.6 %copy-start.21 = (bf16[256,1024]{1,0:T(8,128)(2,1)S(1)}, bf16[256,1024]{1,0:T(8,128)(2,1)}, u32[]{:S(2)}) copy-start(bf16[256,1024]{1,0:T(8,128)(2,1)} %param.18) | copy-start | bytes 1572868
  159.1 3.6 %copy-start.23 = (f32[256]{0:T(256)S(1)}, f32[256]{0:T(256)}, u32[]{:S(2)}) copy-start(f32[256]{0:T(256)} %param.20) | copy-start | bytes 3076
  162.7 1.0 copy-start.15
  162.7 1.1 copy-start.16
  163.5 0.6 copy-start.18
  164.8 16.2 %copy-start.20 = (s32[8]{0:T(128)S(1)}, s32[8]{0:T(128)}, u32[]{:S(2)}) copy-start(s32[8]{0:T(128)} %copy-done.19) | copy-start | bytes 100
  181.0 0.9 copy-start.5
  181.0 1.1 copy-start.6
  182.3 9.3 %collective-permute-start.12 = (bf16[1,2,1,128,512]{4,3,1,2,0:T(8,128)(2,1)S(1)}, bf16[1,2,1,128,512]{4,3,1,2,0:T(8,128)(2,1)S(1)}, u32[]{:S(2)}, u32[]{:S(2)}) collective-permute-start(bf16[1,2,1,128,512]{4,3,1,2,0:T(8,128)(2,1)S(1)} %pad_maximum_fusion.21), channel_id=1, source_target_pairs={{0,128},{128,256},{256,384},{1,129},{129,257},{257,385},{2,130},{1... | collective-permute-start | bytes 786440 | tf_op jit(solution)/shard_map/ppermute | solution.py:21
  186.9 29.9 %collective-permute-start.13 = (bf16[1,2,1,128,512]{4,3,1,2,0:T(8,128)(2,1)S(1)}, bf16[1,2,1,128,512]{4,3,1,2,0:T(8,128)(2,1)S(1)}, u32[]{:S(2)}, u32[]{:S(2)}) collective-permute-start(bf16[1,2,1,128,512]{4,3,1,2,0:T(8,128)(2,1)S(1)} %pad_maximum_fusion.21), channel_id=1, source_target_pairs={{128,0},{256,128},{384,256},{129,1},{257,129},{385,257},{130,2},{2... | collective-permute-start | bytes 786440 | tf_op jit(solution)/shard_map/ppermute | solution.py:23
  217.0 24.3 %copy-start.8 = (bf16[256,256]{1,0:T(8,128)(2,1)S(1)}, bf16[256,256]{1,0:T(8,128)(2,1)}, u32[]{:S(2)}) copy-start(bf16[256,256]{1,0:T(8,128)(2,1)} %param.14) | copy-start | bytes 393220
  217.0 12.2 %collective-permute-start.14 = (bf16[3,1,1,128,512]{4,3,1,2,0:T(8,128)(2,1)S(1)}, bf16[3,1,1,128,512]{4,3,1,2,0:T(8,128)(2,1)S(1)}, u32[]{:S(2)}, u32[]{:S(2)}) collective-permute-start(bf16[3,1,1,128,512]{4,3,1,2,0:T(8,128)(2,1)S(1)} %get-tuple-element.14), channel_id=1, source_target_pairs={{0,8},{8,16},{16,24},{24,32},{32,40},{40,48},{48,56},{56,64},{64,7... | collective-permute-start | bytes 1179656 | tf_op jit(solution)/shard_map/ppermute | solution.py:21
  221.0 13.9 %collective-permute-start.15 = (bf16[3,1,1,128,512]{4,3,1,2,0:T(8,128)(2,1)S(1)}, bf16[3,1,1,128,512]{4,3,1,2,0:T(8,128)(2,1)S(1)}, u32[]{:S(2)}, u32[]{:S(2)}) collective-permute-start(bf16[3,1,1,128,512]{4,3,1,2,0:T(8,128)(2,1)S(1)} %get-tuple-element.13), channel_id=1, source_target_pairs={{8,0},{16,8},{24,16},{32,24},{40,32},{48,40},{56,48},{64,56},{72,6... | collective-permute-start | bytes 1179656 | tf_op jit(solution)/shard_map/ppermute | solution.py:23
  229.2 12.9 %copy-start.2 = (bf16[3,1,1,128,512]{4,3,1,2,0:T(8,128)(2,1)}, bf16[3,1,1,128,512]{4,3,1,2,0:T(8,128)(2,1)S(1)}, u32[]{:S(2)}) copy-start(bf16[3,1,1,128,512]{4,3,1,2,0:T(8,128)(2,1)S(1)} %collective-permute-done.14) | copy-start | bytes 1179652
  235.0 19.3 %collective-permute-start.16 = (bf16[3,4,1,128,512]{4,3,1,2,0:T(8,128)(2,1)S(1)}, bf16[3,4,1,128,512]{4,3,1,2,0:T(8,128)(2,1)}, u32[]{:S(2)}, u32[]{:S(2)}) collective-permute-start(bf16[3,4,1,128,512]{4,3,1,2,0:T(8,128)(2,1)S(1)} %pad_maximum_fusion.1), channel_id=1, source_target_pairs={{0,1},{1,2},{2,3},{3,4},{4,5},{5,6},{6,7},{8,9},{9,10},{10,11},{11... | collective-permute-start | bytes 4718600 | tf_op jit(solution)/shard_map/ppermute | solution.py:21
  236.9 21.8 %collective-permute-start.17 = (bf16[3,4,1,128,512]{4,3,1,2,0:T(8,128)(2,1)S(1)}, bf16[3,4,1,128,512]{4,3,1,2,0:T(8,128)(2,1)}, u32[]{:S(2)}, u32[]{:S(2)}) collective-permute-start(bf16[3,4,1,128,512]{4,3,1,2,0:T(8,128)(2,1)S(1)} %pad_maximum_fusion.1), channel_id=1, source_target_pairs={{1,0},{2,1},{3,2},{4,3},{5,4},{6,5},{7,6},{9,8},{10,9},{11,10},{12... | collective-permute-start | bytes 4718600 | tf_op jit(solution)/shard_map/ppermute | solution.py:23
  245.3 1.0 copy-start.3
  260.1 0.8 copy-start.14
  267.0 0.9 copy-start.13
  271.1 3.0 %copy-start.10 = (bf16[256,256]{1,0:T(8,128)(2,1)S(1)}, bf16[256,256]{1,0:T(8,128)(2,1)}, u32[]{:S(2)}) copy-start(bf16[256,256]{1,0:T(8,128)(2,1)} %param.17) | copy-start | bytes 393220
  271.1 3.6 %copy-start.22 = (bf16[256,1024]{1,0:T(8,128)(2,1)S(1)}, bf16[256,1024]{1,0:T(8,128)(2,1)}, u32[]{:S(2)}) copy-start(bf16[256,1024]{1,0:T(8,128)(2,1)} %param.18) | copy-start | bytes 1572868
  271.1 3.6 %copy-start.24 = (f32[256]{0:T(256)S(1)}, f32[256]{0:T(256)}, u32[]{:S(2)}) copy-start(f32[256]{0:T(256)} %param.20) | copy-start | bytes 3076
where the time goes:
time: 278 us; the launch traced here: 277 us
  starting transfers between devices  97.5 us (35%)
  waiting for transfers between devices  87.3 us (31%)
  local copies, waits for them, and re-layouts  33.6 us (12%)
  matrix products  29.6 us (11%)
  blocking collectives  16 us (6%)
  other arithmetic  11.6 us (4%)
    ppermute x12, starting transfers between devices, padded_2(): lax.ppermute(tail, axis, [(i, (i + 1) % count) for i in range(ends)])  63.4 us
    ppermute x12, waiting for transfers between devices, padded_2(): lax.ppermute(head, axis, [((i + 1) % count, i) for i in range(ends)])  54.8 us
    ppermute x12, waiting for transfers between devices, padded_2(): lax.ppermute(tail, axis, [(i, (i + 1) % count) for i in range(ends)])  28.8 us
    ppermute x12, starting transfers between devices, padded_2(): lax.ppermute(head, axis, [((i + 1) % count, i) for i in range(ends)])  24.9 us
    all_to_all x1, blocking collectives, relocate(): lax.all_to_all(outgoing.astype(jnp.bfloat16), 'gz', split_axis=0, concat_...  16 us
    sub x4, matrix products, attend(): weights = jnp.where(valid, jnp.exp(scores - peak), 0.0)  13 us
    another operation x22, local copies, waits for them, and re-layouts, neighbours(): return jnp.stack(parts, axis=3)  11.7 us
    dot_general x4, matrix products, attend(): jnp.einsum('bhqk,bkhd->bqhd', weights, value_heads, preferred_element_typ...  11.6 us
  transfers between devices with their start and end apart: 26, of which 14 were waited for; matrix products, arithmetic and copies ran while one was open for 11% of the time, Pallas kernels for 0%

commit v1 on v0

v1 whole, which is shorter than its diff:
```python
import functools
import math

import jax
import jax.numpy as jnp
from jax import lax
from jax.experimental import pallas as pl
from jax.experimental.pallas import tpu as pltpu
from jax.sharding import PartitionSpec as P

MESH = pl.DeviceIdType.MESH
HEADS = 8
EPSILON = 1e-05
SLOTS = 128
WIDTH = 256
HEAD = WIDTH // HEADS
FF = 1024
MARK = 2.0**20
LIMIT = 2.0**19
NEGATIVE = -1e30
SCALE = HEAD**-0.5 * math.log2(math.e)

Y_LOW, Z0_LOW, Z0_HIGH, OWN0, OWN1, Z1_LOW, Z1_HIGH, Y_HIGH, X_FIRST = range(9)
Z_LOW, Z_HIGH = (Z0_LOW, Z1_LOW), (Z0_HIGH, Z1_HIGH)
NEAR = 5 * SLOTS
FAR = 2 * SLOTS
PAIRS = HEADS // 2


def nt(left, right):
    return lax.dot_general(left, right, (((1,), (1,)), ((), ())), preferred_element_type=jnp.float32)


def nn(left, right):
    return jnp.dot(left, right, preferred_element_type=jnp.float32)


def layer_norm(values, gain):
    centre = values - jnp.mean(values, axis=-1, keepdims=True)
    spread = jnp.mean(centre * centre, axis=-1, keepdims=True)
    return centre * lax.rsqrt(spread + EPSILON) * gain


def gelu(x):
    return 0.5 * x * (1.0 + jnp.tanh(math.sqrt(2.0 / math.pi) * (x + 0.044715 * (x * x * x))))


def marked(rows, live):
    return jnp.where(live, rows, MARK).astype(jnp.bfloat16)


def penalty(rows):
    first = (lax.broadcasted_iota(jnp.int32, (8, WIDTH), 1) == 0).astype(jnp.bfloat16)
    return jnp.where(nt(first, rows) > LIMIT, NEGATIVE, 0.0)


def kernel(
    features, occupancy, dest_bin, wq, wk, wv, wo, wu, wd, ga, gf, out,
    state, q_w, k_w, v_w, o_w, u_w, d_w, a_g, f_g,
    rows1, rows2, line, places, q_stack, keys, values, far_keys, far_values,
    near_pen, far_pen, peak, total, mixed, result,
    load_sem, out_sem,
    x_send, x_recv, y_send, y_recv, z_send, z_recv, p_send, p_recv,
    m_send, m_recv, s_send, s_recv,
):
    x, y, z = lax.axis_index("gx"), lax.axis_index("gy"), lax.axis_index("gz")
    nx, ny, nz = lax.axis_size("gx"), lax.axis_size("gy"), lax.axis_size("gz")
    chips = nz // 2
    chip, core = z // 2, z % 2
    twin = (x, y, chip * 2 + (1 - core))

    def around(step):
        return (x, y, lax.rem(z + step, nz))

    def other_chip(step):
        return (x, y, lax.rem(chip + step, chips) * 2 + core)

    has = {
        ("x", 0): x > 0, ("x", 1): x < nx - 1,
        ("y", 0): y > 0, ("y", 1): y < ny - 1,
        ("z", 0): z > 0, ("z", 1): z < nz - 1,
    }
    peer = {
        ("x", 0): (jnp.maximum(x - 1, 0), y, z), ("x", 1): (jnp.minimum(x + 1, nx - 1), y, z),
        ("y", 0): (x, jnp.maximum(y - 1, 0), z), ("y", 1): (x, jnp.minimum(y + 1, ny - 1), z),
        ("z", 0): (x, y, jnp.maximum(z - 1, 0)), ("z", 1): (x, y, jnp.minimum(z + 1, nz - 1)),
    }

    loads = [
        pltpu.make_async_copy(source, target, load_sem.at[i])
        for i, (source, target) in enumerate(
            [
                (features, state), (wq, q_w), (wk, k_w), (wv, v_w), (wo, o_w), (wu, u_w),
                (wd, d_w), (ga, a_g), (gf, f_g),
            ]
        )
    ]
    for load in loads:
        load.start()

    barrier = pltpu.get_barrier_semaphore()
    for step in range(1, nz):
        pl.semaphore_signal(barrier, inc=1, device_id=around(step), device_id_type=MESH)
    for axis in "xy":
        for side in (0, 1):

            @pl.when(has[axis, side])
            def _():
                pl.semaphore_signal(barrier, inc=1, device_id=peer[axis, side], device_id_type=MESH)

    row_id = lax.broadcasted_iota(jnp.int32, (SLOTS, WIDTH), 0)
    tile_row = lax.broadcasted_iota(jnp.int32, (8, 128), 0)
    places[z] = jnp.where(
        tile_row == 0, dest_bin[0], jnp.where(tile_row == 1, dest_bin[1], -1)
    )
    loads[0].wait()
    for b in range(2):
        rows1[OWN0 + b] = marked(state[b], row_id < occupancy[b])

    dead = jnp.full((SLOTS, WIDTH), MARK, jnp.bfloat16)
    for rows in (rows1, rows2):
        for side in (0, 1):

            @pl.when(jnp.logical_not(has["x", side]))
            def _():
                for b in range(2):
                    rows[X_FIRST + 2 * b + side] = dead

            @pl.when(jnp.logical_not(has["y", side]))
            def _():
                rows[(Y_LOW, Y_HIGH)[side]] = dead

    for side in (0, 1):

        @pl.when(jnp.logical_not(has["z", side]))
        def _():
            for b in range(2):
                rows1[(Z_LOW, Z_HIGH)[side][b]] = dead

    greeted = sum((has[axis, side].astype(jnp.int32) for axis in "xy" for side in (0, 1)), nz - 1)
    pl.semaphore_wait(barrier, greeted)

    def x_copy(layer, rows, b, side):
        return pltpu.make_async_remote_copy(
            src_ref=rows.at[OWN0 + b],
            dst_ref=rows.at[X_FIRST + 2 * b + (1 - side)],
            send_sem=x_send.at[layer, b, side],
            recv_sem=x_recv.at[layer, b, 1 - side],
            device_id=peer["x", side],
            device_id_type=MESH,
        )

    def y_copy(layer, rows, side):
        return pltpu.make_async_remote_copy(
            src_ref=rows.at[OWN0 + side],
            dst_ref=rows.at[(Y_LOW, Y_HIGH)[1 - side]],
            send_sem=y_send.at[layer, side],
            recv_sem=y_recv.at[layer, 1 - side],
            device_id=peer["y", side],
            device_id_type=MESH,
        )

    def z_copy(b, side):
        return pltpu.make_async_remote_copy(
            src_ref=rows1.at[OWN0 + b],
            dst_ref=rows1.at[(Z_LOW, Z_HIGH)[1 - side][b]],
            send_sem=z_send.at[b, side],
            recv_sem=z_recv.at[b, 1 - side],
            device_id=peer["z", side],
            device_id_type=MESH,
        )

    def place_copy(step):
        return pltpu.make_async_remote_copy(
            src_ref=places.at[z],
            dst_ref=places.at[z],
            send_sem=p_send.at[step - 1],
            recv_sem=p_recv.at[step - 1],
            device_id=around(step),
            device_id_type=MESH,
        )

    def line_copy(b, step):
        own = line.at[2 * z + b]
        return pltpu.make_async_remote_copy(
            src_ref=own,
            dst_ref=own,
            send_sem=m_send.at[b, step - 1],
            recv_sem=m_recv.at[b, step - 1],
            device_id=other_chip(step),
            device_id_type=MESH,
        )

    def twin_copy(b, step):
        origin = lax.rem(chip - step + chips, chips) * 2 + core
        block = line.at[2 * origin + b]
        return pltpu.make_async_remote_copy(
            src_ref=block,
            dst_ref=block,
            send_sem=s_send.at[b, step],
            recv_sem=s_recv.at[b, step],
            device_id=twin,
            device_id_type=MESH,
        )

    def on(axis, side, act):
        pl.when(has[axis, side])(act)

    for b in range(2):
        for side in (0, 1):
            on("x", side, lambda: x_copy(0, rows1, b, side).start())
        if b == 0:
            for side in (0, 1):
                on("z", side, lambda: z_copy(0, side).start())
                on("z", side, lambda: z_copy(1, side).start())
                on("y", side, lambda: y_copy(0, rows1, side).start())
    for step in range(1, nz):
        place_copy(step).start()
    for load in loads[1:]:
        load.wait()

    lane = lax.broadcasted_iota(jnp.int32, (SLOTS, WIDTH), 1)

    def project(rows, first, count, key_ref, value_ref):
        block = rows[first : first + count].reshape(count * SLOTS, WIDTH)
        key_ref[...] = nn(block, k_w[...]).astype(jnp.bfloat16)
        value_ref[...] = nn(block, v_w[...]).astype(jnp.bfloat16)
        return penalty(block)

    def project_near(rows):
        query = nn(rows[OWN0 : OWN1 + 1].reshape(2 * SLOTS, WIDTH), q_w[...]).astype(jnp.bfloat16)
        for h in range(HEADS):
            inside = (lane >= h * HEAD) & (lane < (h + 1) * HEAD)
            for b in range(2):
                q_stack[b, h * SLOTS : (h + 1) * SLOTS, :] = jnp.where(
                    inside, query[b * SLOTS : (b + 1) * SLOTS], jnp.bfloat16(0.0)
                )
        near_pen[...] = project(rows, 0, 8, keys, values)

    def attend_near(b):
        first = b * 3 * SLOTS
        key = keys.at[first : first + NEAR, :]
        value = values.at[first : first + NEAR, :]
        pen = near_pen[0:1, first : first + NEAR]

        def pair(g, carry):
            here = pl.ds(pl.multiple_of(g * 2 * SLOTS, 2 * SLOTS), 2 * SLOTS)
            scores = nt(q_stack[b, here, :], key[...]) * SCALE + pen
            top = jnp.max(scores, axis=-1, keepdims=True)
            power = jnp.exp2(scores - top)
            peak[b, here, :] = jnp.broadcast_to(top, (2 * SLOTS, 128))
            total[b, here, :] = jnp.broadcast_to(
                jnp.sum(power, axis=-1, keepdims=True), (2 * SLOTS, 128)
            )
            mixed[b, here, :] = nn(power.astype(jnp.bfloat16), value[...])
            return carry

        lax.fori_loop(0, PAIRS, pair, 0)

    def finish(rows, b, previous):
        far_pen[...] = project(rows, X_FIRST + 2 * b, 2, far_keys, far_values)
        pen = far_pen[0:1, :]
        attended = jnp.zeros((SLOTS, WIDTH), jnp.float32)
        for g in range(PAIRS):
            here = slice(g * 2 * SLOTS, (g + 1) * 2 * SLOTS)
            scores = nt(q_stack[b, here, :], far_keys[...]) * SCALE + pen
            old = peak[b, here, :][:, 0:1]
            top = jnp.maximum(jnp.max(scores, axis=-1, keepdims=True), old)
            power = jnp.exp2(scores - top)
            shrink = jnp.exp2(old - top)
            whole = total[b, here, :][:, 0:1] * shrink + jnp.sum(power, axis=-1, keepdims=True)
            both = mixed[b, here, :] * shrink + nn(power.astype(jnp.bfloat16), far_values[...])
            both = both / whole
            for i in range(2):
                h = 2 * g + i
                inside = (lane >= h * HEAD) & (lane < (h + 1) * HEAD)
                attended = jnp.where(inside, both[i * SLOTS : (i + 1) * SLOTS], attended)
        hidden = layer_norm(previous + nn(attended.astype(jnp.bfloat16), o_w[...]), a_g[...])
        inner = gelu(nn(hidden.astype(jnp.bfloat16), u_w[...])).astype(jnp.bfloat16)
        return layer_norm(hidden + nn(inner, d_w[...]), f_g[...])

    for side in (0, 1):
        for b in range(2):
            on("z", 1 - side, lambda: z_copy(b, side).wait_recv())
        on("y", 1 - side, lambda: y_copy(0, rows1, side).wait_recv())
    project_near(rows1)
    for b in range(2):
        attend_near(b)

    for step in range(1, nz):
        place_copy(step).wait_recv()
    wide = (nz, 8, 128)
    source_id = 2 * lax.broadcasted_iota(jnp.int32, wide, 0) + lax.broadcasted_iota(jnp.int32, wide, 1)
    table = places[...]

    def source(z_at, b):
        flat = (x * (2 * ny) + 2 * y + b) * nz + z_at
        found = jnp.max(jnp.where(table == flat, source_id, 0))
        return jnp.clip(found, 0, 2 * nz - 1)

    z_below, z_above = jnp.maximum(z - 1, 0), jnp.minimum(z + 1, nz - 1)
    origin = [[source(at, b) for b in range(2)] for at in (z_below, z, z_above)]

    for b in range(2):
        for side in (0, 1):
            on("x", 1 - side, lambda: x_copy(0, rows1, b, side).wait_recv())
        updated = finish(rows1, b, state[b])
        line[2 * z + b] = marked(updated, row_id < occupancy[b])
        for step in range(1, chips):
            line_copy(b, step).start()
        twin_copy(b, 0).start()

    for b in range(2):
        for step in range(1, chips):
            line_copy(b, step).wait_recv()
            twin_copy(b, step).start()
    for b in range(2):
        for step in range(chips):
            twin_copy(b, step).wait_recv()

    for b in range(2):
        rows2[OWN0 + b] = line[origin[1][b]]
        for side in (0, 1):
            on("x", side, lambda: x_copy(1, rows2, b, side).start())
    for side in (0, 1):
        on("y", side, lambda: y_copy(1, rows2, side).start())
    for b in range(2):
        for side, at in ((0, 0), (1, 2)):
            slot = (Z_LOW, Z_HIGH)[side][b]
            rows2[slot] = jnp.where(has["z", side], line[origin[at][b]], dead)
    for side in (0, 1):
        on("y", 1 - side, lambda: y_copy(1, rows2, side).wait_recv())
    project_near(rows2)
    for b in range(2):
        attend_near(b)
    for b in range(2):
        for side in (0, 1):
            on("x", 1 - side, lambda: x_copy(1, rows2, b, side).wait_recv())
        own = rows2[OWN0 + b].astype(jnp.float32)
        result[b] = jnp.where(own < LIMIT, finish(rows2, b, own), 0.0)
        pltpu.make_async_copy(result.at[b], out.at[b], out_sem.at[b]).start()

    for side in (0, 1):
        for b in range(2):
            on("x", side, lambda: x_copy(0, rows1, b, side).wait_send())
            on("x", side, lambda: x_copy(1, rows2, b, side).wait_send())
            on("z", side, lambda: z_copy(b, side).wait_send())
        on("y", side, lambda: y_copy(0, rows1, side).wait_send())
        on("y", side, lambda: y_copy(1, rows2, side).wait_send())
    for step in range(1, nz):
        place_copy(step).wait_send()
    for b in range(2):
        for step in range(1, chips):
            line_copy(b, step).wait_send()
        for step in range(chips):
            twin_copy(b, step).wait_send()
        pltpu.make_async_copy(result.at[b], out.at[b], out_sem.at[b]).wait()


def shards(features, occupancy, dest_bin, wq, wk, wv, wo, wu, wd, ga, gf):
    nz = lax.axis_size("gz")
    bf16, f32 = jnp.bfloat16, jnp.float32
    dma = pltpu.SemaphoreType.DMA
    block = (SLOTS, WIDTH)
    anywhere, smem = pl.BlockSpec(memory_space=pl.ANY), pl.BlockSpec(memory_space=pltpu.SMEM)
    out = pl.pallas_call(
        kernel,
        out_shape=jax.ShapeDtypeStruct((2, *block), f32),
        in_specs=[anywhere, smem, smem] + [anywhere] * 8,
        out_specs=anywhere,
        scratch_shapes=[
            pltpu.VMEM((2, *block), f32),
            *[pltpu.VMEM((WIDTH, WIDTH), bf16)] * 4,
            pltpu.VMEM((WIDTH, FF), bf16),
            pltpu.VMEM((FF, WIDTH), bf16),
            pltpu.VMEM((1, WIDTH), f32),
            pltpu.VMEM((1, WIDTH), f32),
            pltpu.VMEM((12, *block), bf16),
            pltpu.VMEM((12, *block), bf16),
            pltpu.VMEM((2 * nz, *block), bf16),
            pltpu.VMEM((nz, 8, 128), jnp.int32),
            pltpu.VMEM((2, HEADS * SLOTS, WIDTH), bf16),
            pltpu.VMEM((8 * SLOTS, WIDTH), bf16),
            pltpu.VMEM((8 * SLOTS, WIDTH), bf16),
            pltpu.VMEM((FAR, WIDTH), bf16),
            pltpu.VMEM((FAR, WIDTH), bf16),
            pltpu.VMEM((8, 8 * SLOTS), f32),
            pltpu.VMEM((8, FAR), f32),
            pltpu.VMEM((2, HEADS * SLOTS, 128), f32),
            pltpu.VMEM((2, HEADS * SLOTS, 128), f32),
            pltpu.VMEM((2, HEADS * SLOTS, WIDTH), f32),
            pltpu.VMEM((2, *block), f32),
            dma((9,)),
            dma((2,)),
            dma((2, 2, 2)),
            dma((2, 2, 2)),
            dma((2, 2)),
            dma((2, 2)),
            dma((2, 2)),
            dma((2, 2)),
            dma((nz - 1,)),
            dma((nz - 1,)),
            dma((2, nz // 2 - 1)),
            dma((2, nz // 2 - 1)),
            dma((2, nz // 2)),
            dma((2, nz // 2)),
        ],
        compiler_params=pltpu.CompilerParams(
            collective_id=0, has_side_effects=True, vmem_limit_bytes=60 << 20
        ),
        name="evolve",
    )(
        features.reshape(2, *block),
        occupancy.reshape(2),
        dest_bin.reshape(2),
        wq, wk, wv, wo, wu, wd,
        ga.reshape(1, WIDTH),
        gf.reshape(1, WIDTH),
    )
    return out.reshape(features.shape)


def solution(mesh):
    cells = P("gx", "gy", "gz")
    return jax.shard_map(
        shards,
        mesh=mesh,
        in_specs=(P("gx", "gy", "gz", None, None), cells, cells) + (P(),) * 8,
        out_specs=P("gx", "gy", "gz", None, None),
        check_vma=False,
    )
```

time: 278 us -> 66.6 us (0.24)
  the two profiles are of different devices: /device:TPU:23 before, /device:TPU:6 now
where the time goes in v1:
time: 66.6 us; the launch traced here: 66.4 us
  Pallas kernels  64.7 us (97%)
  local copies, waits for them, and re-layouts  1.67 us (3%)
    pallas_call x1, Pallas kernels, shards(): pl.pallas_call(kernel, out_shape=jax.ShapeDtypeStruct((2, *block), f32),...  64.7 us
    unnamed x1, local copies, waits for them, and re-layouts  1.67 us

profile of v1, /device:TPU:6, one launch (start us, length us, event | category | flops | bytes accessed | tf_op | source)
XLA Modules:
  0.0 66.4 jit_solution(6454096150529466612)
XLA Ops:
  0.0 64.7 %evolve.1 = f32[2,128,256]{2,1,0:T(8,128)} custom-call(f32[2,128,256]{2,1,0:T(8,128)} %bitcast.9, s32[2]{0:T(128)} %bitcast.12, s32[2]{0:T(128)} %bitcast.13, bf16[256,256]{1,0:T(8,128)(2,1)} %wq.1, bf16[256,256]{1,0:T(8,128)(2,1)} %wk.1, bf16[256,256]{1,0:T(8,128)(2,1)} %wv.1, bf16[256,256]{1,0:T(8,128)(2,1)} %wo.1, bf16[256,1024]{1,0:T(8,128)(2,1)} %wu.1, ...), custom_call_target="tpu_custom_call" | custom-call | tf_op jit(solution)/shard_map/evolve/pallas_call | solution.py:366
  64.7 1.7 %copy.14 = f32[1,2,1,128,256]{4,3,2,1,0:T(8,128)} copy(f32[1,2,1,128,256]{4,3,2,1,0:T(8,128)} %bitcast.8) | data formatting | bytes 524288

commit v2 on v1

v2 whole, which is shorter than its diff:
```python
import functools
import math

import jax
import jax.numpy as jnp
from jax import lax
from jax.experimental import pallas as pl
from jax.experimental.pallas import tpu as pltpu
from jax.sharding import PartitionSpec as P

MESH = pl.DeviceIdType.MESH
HEADS = 8
EPSILON = 1e-05
SLOTS = 128
WIDTH = 256
HEAD = WIDTH // HEADS
FF = 1024
MARK = 2.0**20
LIMIT = 2.0**19
NEGATIVE = -1e30
SCALE = HEAD**-0.5 * math.log2(math.e)

Y_LOW, Z0_LOW, Z0_HIGH, OWN0, OWN1, Z1_LOW, Z1_HIGH, Y_HIGH, X_FIRST = range(9)
Z_LOW, Z_HIGH = (Z0_LOW, Z1_LOW), (Z0_HIGH, Z1_HIGH)
NEAR = 5 * SLOTS
PAIRS = HEADS // 2
UNROLL = 4
RELAY = True
HALF = SLOTS // 2
PIECES = ((0, 0), (0, 1), (1, 0), (1, 1))


def nt(left, right):
    return lax.dot_general(left, right, (((1,), (1,)), ((), ())), preferred_element_type=jnp.float32)


def nn(left, right):
    return jnp.dot(left, right, preferred_element_type=jnp.float32)


def layer_norm(values, gain):
    centre = values - jnp.mean(values, axis=-1, keepdims=True)
    spread = jnp.mean(centre * centre, axis=-1, keepdims=True)
    return centre * lax.rsqrt(spread + EPSILON) * gain


def gelu(x):
    return 0.5 * x * (1.0 + jnp.tanh(math.sqrt(2.0 / math.pi) * (x + 0.044715 * (x * x * x))))


def marked(rows, live):
    return jnp.where(live, rows, MARK).astype(jnp.bfloat16)


def penalty(rows):
    return jnp.where(rows[:, :SLOTS].astype(jnp.float32) > LIMIT, NEGATIVE, 0.0)


def twice(columns):
    return jnp.concatenate([columns, columns], axis=1)


def kernel(
    features, occupancy, dest_bin, wq, wk, wv, wo, wu, wd, ga, gf, out,
    state, q_w, k_w, v_w, o_w, u_w, d_w, a_g, f_g,
    rows1, rows2, line_low, line_high, places, qt_w, vt_w, q_stack, keys, values, near_pen, peak, total, mixed, result,
    load_sem, out_sem,
    x_send, x_recv, y_send, y_recv, z_send, z_recv, p_send, p_recv,
    m_send, m_recv, r_send, s_send, s_recv,
):
    x, y, z = lax.axis_index("gx"), lax.axis_index("gy"), lax.axis_index("gz")
    nx, ny, nz = lax.axis_size("gx"), lax.axis_size("gy"), lax.axis_size("gz")
    chips = nz // 2
    line = (line_low, line_high)
    chip, core = z // 2, z % 2
    twin = (x, y, chip * 2 + (1 - core))

    def around(step):
        return (x, y, lax.rem(z + step, nz))

    def other_chip(step):
        return (x, y, lax.rem(chip + step, chips) * 2 + core)

    has = {
        ("x", 0): x > 0, ("x", 1): x < nx - 1,
        ("y", 0): y > 0, ("y", 1): y < ny - 1,
        ("z", 0): z > 0, ("z", 1): z < nz - 1,
    }
    peer = {
        ("x", 0): (jnp.maximum(x - 1, 0), y, z), ("x", 1): (jnp.minimum(x + 1, nx - 1), y, z),
        ("y", 0): (x, jnp.maximum(y - 1, 0), z), ("y", 1): (x, jnp.minimum(y + 1, ny - 1), z),
        ("z", 0): (x, y, jnp.maximum(z - 1, 0)), ("z", 1): (x, y, jnp.minimum(z + 1, nz - 1)),
    }

    loads = [
        pltpu.make_async_copy(source, target, load_sem.at[i])
        for i, (source, target) in enumerate(
            [
                (features, state), (wq, q_w), (wk, k_w), (wv, v_w), (wo, o_w), (wu, u_w),
                (wd, d_w), (ga, a_g), (gf, f_g),
            ]
        )
    ]
    for load in loads:
        load.start()

    barrier = pltpu.get_barrier_semaphore()
    for step in range(1, nz):
        pl.semaphore_signal(barrier, inc=1, device_id=around(step), device_id_type=MESH)
    for axis in "xy":
        for side in (0, 1):

            @pl.when(has[axis, side])
            def _():
                pl.semaphore_signal(barrier, inc=1, device_id=peer[axis, side], device_id_type=MESH)

    row_id = lax.broadcasted_iota(jnp.int32, (SLOTS, WIDTH), 0)
    tile_row = lax.broadcasted_iota(jnp.int32, (8, 128), 0)
    places[z] = jnp.where(
        tile_row == 0, dest_bin[0], jnp.where(tile_row == 1, dest_bin[1], -1)
    )
    loads[0].wait()
    for b in range(2):
        rows1[OWN0 + b] = marked(state[b], row_id < occupancy[b])

    dead = jnp.full((SLOTS, WIDTH), MARK, jnp.bfloat16)
    for rows in (rows1, rows2):
        for side in (0, 1):

            @pl.when(jnp.logical_not(has["y", side]))
            def _():
                rows[(Y_LOW, Y_HIGH)[side]] = dead

    for side in (0, 1):

        @pl.when(jnp.logical_not(has["z", side]))
        def _():
            for b in range(2):
                rows1[(Z_LOW, Z_HIGH)[side][b]] = dead

    greeted = sum((has[axis, side].astype(jnp.int32) for axis in "xy" for side in (0, 1)), nz - 1)
    pl.semaphore_wait(barrier, greeted)

    def x_copy(rows, b, side, half=None):
        span = slice(0, SLOTS) if half is None else slice(half * HALF, (half + 1) * HALF)
        number = 0 if half is None else 1 + half
        return pltpu.make_async_remote_copy(
            src_ref=rows.at[OWN0 + b, span],
            dst_ref=rows.at[X_FIRST + 2 * b + (1 - side), span],
            send_sem=x_send.at[number, b, side],
            recv_sem=x_recv.at[number, b, 1 - side],
            device_id=peer["x", side],
            device_id_type=MESH,
        )

    def y_copy(layer, rows, side):
        return pltpu.make_async_remote_copy(
            src_ref=rows.at[OWN0 + side],
            dst_ref=rows.at[(Y_LOW, Y_HIGH)[1 - side]],
            send_sem=y_send.at[layer, side],
            recv_sem=y_recv.at[layer, 1 - side],
            device_id=peer["y", side],
            device_id_type=MESH,
        )

    def z_copy(b, side):
        return pltpu.make_async_remote_copy(
            src_ref=rows1.at[OWN0 + b],
            dst_ref=rows1.at[(Z_LOW, Z_HIGH)[1 - side][b]],
            send_sem=z_send.at[b, side],
            recv_sem=z_recv.at[b, 1 - side],
            device_id=peer["z", side],
            device_id_type=MESH,
        )

    def place_copy(step):
        return pltpu.make_async_remote_copy(
            src_ref=places.at[z],
            dst_ref=places.at[z],
            send_sem=p_send.at[step - 1],
            recv_sem=p_recv.at[step - 1],
            device_id=around(step),
            device_id_type=MESH,
        )

    def part(origin, piece):
        b, half = PIECES[piece]
        return line[half].at[2 * origin + b]

    def line_copy(piece, step):
        own = part(z, piece)
        return pltpu.make_async_remote_copy(
            src_ref=own,
            dst_ref=own,
            send_sem=m_send.at[piece, step - 1],
            recv_sem=m_recv.at[piece, step - 1],
            device_id=other_chip(step),
            device_id_type=MESH,
        )

    def relay_copy(piece):
        block = part(lax.rem(chip + 2, chips) * 2 + core, piece)
        upward = chip == 2
        return pltpu.make_async_remote_copy(
            src_ref=block,
            dst_ref=block,
            send_sem=r_send.at[piece],
            recv_sem=m_recv.at[piece, jnp.where(upward, 2, 0)],
            device_id=(x, y, jnp.where(upward, 6, 0) + core),
            device_id_type=MESH,
        )

    def twin_copy(piece, step):
        block = part(lax.rem(chip - step + chips, chips) * 2 + core, piece)
        return pltpu.make_async_remote_copy(
            src_ref=block,
            dst_ref=block,
            send_sem=s_send.at[piece, step],
            recv_sem=s_recv.at[piece, step],
            device_id=twin,
            device_id_type=MESH,
        )

    inner_chip = (chip == 1) | (chip == 2)

    def direct(step, act):
        if step == 2 or not RELAY:
            act()
        else:
            pl.when(chip != (3 if step == 1 else 0))(act)

    def share(piece):
        for step in (2, 1, 3):
            direct(step, lambda: line_copy(piece, step).start())
        twin_copy(piece, 0).start()

    def pass_on(piece):
        line_copy(piece, 2).wait_recv()
        if RELAY:
            pl.when(inner_chip)(lambda: relay_copy(piece).start())
        twin_copy(piece, 2).start()
        for step in (1, 3):
            line_copy(piece, step).wait_recv()
            twin_copy(piece, step).start()

    def arrived(piece):
        for step in range(chips):
            twin_copy(piece, step).wait_recv()

    def on(axis, side, act):
        pl.when(has[axis, side])(act)

    for side in (0, 1):
        on("x", side, lambda: x_copy(rows1, 0, side).start())
    for side in (0, 1):
        for b in range(2):
            on("z", side, lambda: z_copy(b, side).start())
        on("y", side, lambda: y_copy(0, rows1, side).start())
    for step in range(1, nz):
        place_copy(step).start()
    for load in loads[1:]:
        load.wait()

    qt_w[...] = q_w[...].astype(jnp.float32).T.astype(jnp.bfloat16)
    vt_w[...] = v_w[...].astype(jnp.float32).T.astype(jnp.bfloat16)
    for b in range(2):
        q_stack[b] = jnp.zeros((WIDTH, HEADS * SLOTS), jnp.bfloat16)

    def project(rows, first, count):
        block = rows[first : first + count].reshape(count * SLOTS, WIDTH)
        key = nn(block, k_w[...]).astype(jnp.bfloat16)
        value = nt(vt_w[...], block).astype(jnp.bfloat16)
        return key, value, penalty(block)

    def project_near(rows):
        query = nt(qt_w[...], rows[OWN0 : OWN1 + 1].reshape(2 * SLOTS, WIDTH)).astype(jnp.bfloat16)
        for b in range(2):
            for h in range(HEADS):
                down, across = slice(h * HEAD, (h + 1) * HEAD), slice(h * SLOTS, (h + 1) * SLOTS)
                q_stack[b, down, across] = query[down, b * SLOTS : (b + 1) * SLOTS]
        keys[...], values[...], near_pen[...] = project(rows, 0, 8)

    def attend_near(b):
        near = slice(b * 3 * SLOTS, b * 3 * SLOTS + NEAR)

        def pair(g, carry):
            across = pl.ds(pl.multiple_of(g * 2 * SLOTS, 2 * SLOTS), 2 * SLOTS)
            down = pl.ds(pl.multiple_of(g * 2 * HEAD, 2 * HEAD), 2 * HEAD)
            scores = nn(keys[near, :], q_stack[b, :, across]) * SCALE + twice(near_pen[near, :])
            top = jnp.max(scores, axis=0, keepdims=True)
            power = jnp.exp2(scores - top)
            peak[b, g] = top
            total[b, g] = jnp.sum(power, axis=0, keepdims=True)
            both = nn(values[down, near], power.astype(jnp.bfloat16))
            mixed[b, g] = jnp.concatenate([both[:HEAD, :SLOTS], both[HEAD:, SLOTS:]], axis=0)
            return carry

        lax.fori_loop(0, PAIRS, pair, 0, unroll=UNROLL)

    def absorb(rows, b, side):
        key, value, pen = project(rows, X_FIRST + 2 * b + side, 1)
        pen = twice(pen)
        for g in range(PAIRS):
            scores = nn(key, q_stack[b, :, g * 2 * SLOTS : (g + 1) * 2 * SLOTS]) * SCALE + pen
            old = peak[b, g]
            top = jnp.maximum(jnp.max(scores, axis=0, keepdims=True), old)
            power = jnp.exp2(scores - top)
            shrink = jnp.exp2(old - top)
            peak[b, g] = top
            total[b, g] = total[b, g] * shrink + jnp.sum(power, axis=0, keepdims=True)
            both = nn(value[g * 2 * HEAD : (g + 1) * 2 * HEAD, :], power.astype(jnp.bfloat16))
            for i in range(2):
                down, across = slice(i * HEAD, (i + 1) * HEAD), slice(i * SLOTS, (i + 1) * SLOTS)
                mixed[b, g, down, :] = mixed[b, g, down, :] * shrink[:, across] + both[down, across]

    def attended(b):
        pieces = []
        for g in range(PAIRS):
            whole = 1.0 / total[b, g]
            for i in range(2):
                piece = mixed[b, g, i * HEAD : (i + 1) * HEAD, :]
                pieces.append(piece * whole[:, i * SLOTS : (i + 1) * SLOTS])
        return jnp.concatenate(pieces, axis=0)

    def feed(heads, previous):
        weighed = nn(heads.T.astype(jnp.bfloat16), o_w[...])
        hidden = layer_norm(previous + weighed, a_g[...])
        inner = gelu(nn(hidden.astype(jnp.bfloat16), u_w[...])).astype(jnp.bfloat16)
        return layer_norm(hidden + nn(inner, d_w[...]), f_g[...])

    for side in (0, 1):
        for b in range(2):
            on("z", 1 - side, lambda: z_copy(b, side).wait_recv())
        on("y", 1 - side, lambda: y_copy(0, rows1, side).wait_recv())
    project_near(rows1)
    for side in (0, 1):

        @pl.when(has["x", side])
        def _():
            x_copy(rows1, 0, side).wait_send()
            x_copy(rows1, 1, side).start()

    for b in range(2):
        attend_near(b)

    for step in range(1, nz):
        place_copy(step).wait_recv()
    wide = (nz, 8, 128)
    source_id = 2 * lax.broadcasted_iota(jnp.int32, wide, 0) + lax.broadcasted_iota(jnp.int32, wide, 1)
    table = places[...]

    def source(z_at, b):
        flat = (x * (2 * ny) + 2 * y + b) * nz + z_at
        found = jnp.max(jnp.where(table == flat, source_id, 0))
        return jnp.clip(found, 0, 2 * nz - 1)

    z_below, z_above = jnp.maximum(z - 1, 0), jnp.minimum(z + 1, nz - 1)
    origin = [[source(at, b) for b in range(2)] for at in (z_below, z, z_above)]

    for b in range(2):
        for side in (0, 1):

            @pl.when(has["x", side])
            def _():
                x_copy(rows1, b, 1 - side).wait_recv()
                absorb(rows1, b, side)

        updated = feed(attended(b), state[b])
        sent = marked(updated, row_id < occupancy[b])
        for half in range(2):
            line[half][2 * z + b] = sent[half * HALF : (half + 1) * HALF]
            share(2 * b + half)

    pass_on(0)
    pass_on(1)
    pass_on(2)
    arrived(0)
    arrived(2)
    for half in range(2):
        if half == 1:
            pass_on(3)
            arrived(1)
            arrived(3)
        span = slice(half * HALF, (half + 1) * HALF)
        for b in range(2):
            rows2[OWN0 + b, span] = line[half][origin[1][b]]
        for side in (0, 1):

            @pl.when(has["x", side])
            def _():
                for b in range(2):
                    if half == 1:
                        x_copy(rows2, b, side, 0).wait_send()
                    x_copy(rows2, b, side, half).start()

    for side in (0, 1):
        on("y", side, lambda: y_copy(1, rows2, side).start())
    for b in range(2):
        for side, at in ((0, 0), (1, 2)):
            slot = (Z_LOW, Z_HIGH)[side][b]
            for half in range(2):
                span = slice(half * HALF, (half + 1) * HALF)
                rows2[slot, span] = jnp.where(has["z", side], line[half][origin[at][b]], dead[:HALF])
    for side in (0, 1):
        on("y", 1 - side, lambda: y_copy(1, rows2, side).wait_recv())
    project_near(rows2)
    for b in range(2):
        attend_near(b)
    for b in range(2):
        for side in (0, 1):

            @pl.when(has["x", side])
            def _():
                for half in range(2):
                    x_copy(rows2, b, 1 - side, half).wait_recv()
                absorb(rows2, b, side)

    own = rows2[OWN0 : OWN1 + 1].reshape(2 * SLOTS, WIDTH).astype(jnp.float32)
    final = feed(jnp.concatenate([attended(0), attended(1)], axis=1), own)
    result[...] = jnp.where(own < LIMIT, final, 0.0)
    result_copy = pltpu.make_async_copy(result, out, out_sem)
    result_copy.start()

    for side in (0, 1):
        on("x", side, lambda: x_copy(rows1, 1, side).wait_send())
        for b in range(2):
            on("x", side, lambda: x_copy(rows2, b, side, 1).wait_send())
            on("z", side, lambda: z_copy(b, side).wait_send())
        on("y", side, lambda: y_copy(0, rows1, side).wait_send())
        on("y", side, lambda: y_copy(1, rows2, side).wait_send())
    for step in range(1, nz):
        place_copy(step).wait_send()
    for piece in range(len(PIECES)):
        for step in range(1, chips):
            direct(step, lambda: line_copy(piece, step).wait_send())
        if RELAY:
            pl.when(inner_chip)(lambda: relay_copy(piece).wait_send())
        for step in range(chips):
            twin_copy(piece, step).wait_send()
    result_copy.wait()


def shards(features, occupancy, dest_bin, wq, wk, wv, wo, wu, wd, ga, gf):
    nz = lax.axis_size("gz")
    bf16, f32 = jnp.bfloat16, jnp.float32
    dma = pltpu.SemaphoreType.DMA
    block = (SLOTS, WIDTH)
    anywhere, smem = pl.BlockSpec(memory_space=pl.ANY), pl.BlockSpec(memory_space=pltpu.SMEM)
    out = pl.pallas_call(
        kernel,
        out_shape=jax.ShapeDtypeStruct((2 * SLOTS, WIDTH), f32),
        in_specs=[anywhere, smem, smem] + [anywhere] * 8,
        out_specs=anywhere,
        scratch_shapes=[
            pltpu.VMEM((2, *block), f32),
            *[pltpu.VMEM((WIDTH, WIDTH), bf16)] * 4,
            pltpu.VMEM((WIDTH, FF), bf16),
            pltpu.VMEM((FF, WIDTH), bf16),
            pltpu.VMEM((1, WIDTH), f32),
            pltpu.VMEM((1, WIDTH), f32),
            pltpu.VMEM((12, *block), bf16),
            pltpu.VMEM((12, *block), bf16),
            pltpu.VMEM((2 * nz, HALF, WIDTH), bf16),
            pltpu.VMEM((2 * nz, HALF, WIDTH), bf16),
            pltpu.VMEM((nz, 8, 128), jnp.int32),
            pltpu.VMEM((WIDTH, WIDTH), bf16),
            pltpu.VMEM((WIDTH, WIDTH), bf16),
            pltpu.VMEM((2, WIDTH, HEADS * SLOTS), bf16),
            pltpu.VMEM((8 * SLOTS, WIDTH), bf16),
            pltpu.VMEM((WIDTH, 8 * SLOTS), bf16),
            pltpu.VMEM((8 * SLOTS, SLOTS), f32),
            pltpu.VMEM((2, PAIRS, 1, 2 * SLOTS), f32),
            pltpu.VMEM((2, PAIRS, 1, 2 * SLOTS), f32),
            pltpu.VMEM((2, PAIRS, 2 * HEAD, SLOTS), f32),
            pltpu.VMEM((2 * SLOTS, WIDTH), f32),
            dma((9,)),
            dma,
            dma((3, 2, 2)),
            dma((3, 2, 2)),
            dma((2, 2)),
            dma((2, 2)),
            dma((2, 2)),
            dma((2, 2)),
            dma((nz - 1,)),
            dma((nz - 1,)),
            dma((len(PIECES), nz // 2 - 1)),
            dma((len(PIECES), nz // 2 - 1)),
            dma((len(PIECES),)),
            dma((len(PIECES), nz // 2)),
            dma((len(PIECES), nz // 2)),
        ],
        compiler_params=pltpu.CompilerParams(
            collective_id=0, has_side_effects=True, vmem_limit_bytes=60 << 20
        ),
        name="evolve",
    )(
        features.reshape(2, *block),
        occupancy.reshape(2),
        dest_bin.reshape(2),
        wq, wk, wv, wo, wu, wd,
        ga.reshape(1, WIDTH),
        gf.reshape(1, WIDTH),
    )
    return out.reshape(features.shape)


def solution(mesh):
    cells = P("gx", "gy", "gz")
    return jax.shard_map(
        shards,
        mesh=mesh,
        in_specs=(P("gx", "gy", "gz", None, None), cells, cells) + (P(),) * 8,
        out_specs=P("gx", "gy", "gz", None, None),
        check_vma=False,
    )
```

time: 66.6 us -> 61.3 us (0.920)
  the two profiles are of different devices: /device:TPU:6 before, /device:TPU:153 now
where the time goes in v2:
time: 61.3 us; the launch traced here: 61.1 us
  Pallas kernels  59.5 us (97%)
  local copies, waits for them, and re-layouts  1.67 us (3%)
    pallas_call x1, Pallas kernels, shards(): pl.pallas_call(kernel, out_shape=jax.ShapeDtypeStruct((2 * SLOTS, WIDTH),...  59.5 us
    unnamed x1, local copies, waits for them, and re-layouts  1.67 us

profile of v2, /device:TPU:153, one launch (start us, length us, event | category | flops | bytes accessed | tf_op | source)
XLA Modules:
  0.0 61.1 jit_solution(6114216850954452370)
XLA Ops:
  0.0 59.5 %evolve.1 = f32[256,256]{1,0:T(8,128)} custom-call(f32[2,128,256]{2,1,0:T(8,128)} %bitcast.9, s32[2]{0:T(128)} %bitcast.12, s32[2]{0:T(128)} %bitcast.13, bf16[256,256]{1,0:T(8,128)(2,1)} %wq.1, bf16[256,256]{1,0:T(8,128)(2,1)} %wk.1, bf16[256,256]{1,0:T(8,128)(2,1)} %wv.1, bf16[256,256]{1,0:T(8,128)(2,1)} %wo.1, bf16[256,1024]{1,0:T(8,128)(2,1)} %wu.1, ...), custom_call_target="tpu_custom_call" | custom-call | tf_op jit(solution)/shard_map/evolve/pallas_call | solution.py:449
  59.5 1.7 %copy.14 = f32[1,2,1,128,256]{4,3,2,1,0:T(8,128)} copy(f32[1,2,1,128,256]{4,3,2,1,0:T(8,128)} %bitcast.8) | data formatting | bytes 524288

commit v3 on v2

--- a/solution.py
+++ b/solution.py
@@ -365,14 +365,15 @@
                 x_copy(rows1, b, 1 - side).wait_recv()
                 absorb(rows1, b, side)
 
+        if b == 1:
+            pass_on(0)
+            pass_on(1)
         updated = feed(attended(b), state[b])
         sent = marked(updated, row_id < occupancy[b])
         for half in range(2):
             line[half][2 * z + b] = sent[half * HALF : (half + 1) * HALF]
             share(2 * b + half)
 
-    pass_on(0)
-    pass_on(1)
     pass_on(2)
     arrived(0)
     arrived(2)

time: 61.3 us -> 68.1 us (1.11)
  the two profiles are of different devices: /device:TPU:153 before, /device:TPU:6 now
where the time goes in v3:
time: 68.1 us; the launch traced here: 67.5 us
  Pallas kernels  65.8 us (97%)
  local copies, waits for them, and re-layouts  1.67 us (2%)
    pallas_call x1, Pallas kernels, shards(): pl.pallas_call(kernel, out_shape=jax.ShapeDtypeStruct((2 * SLOTS, WIDTH),...  65.8 us
    unnamed x1, local copies, waits for them, and re-layouts  1.67 us

profile of v3, /device:TPU:6, one launch (start us, length us, event | category | flops | bytes accessed | tf_op | source)
XLA Modules:
  0.0 67.5 jit_solution(15510178428497656296)
XLA Ops:
  0.0 65.8 %evolve.1 = f32[256,256]{1,0:T(8,128)} custom-call(f32[2,128,256]{2,1,0:T(8,128)} %bitcast.9, s32[2]{0:T(128)} %bitcast.12, s32[2]{0:T(128)} %bitcast.13, bf16[256,256]{1,0:T(8,128)(2,1)} %wq.1, bf16[256,256]{1,0:T(8,128)(2,1)} %wk.1, bf16[256,256]{1,0:T(8,128)(2,1)} %wv.1, bf16[256,256]{1,0:T(8,128)(2,1)} %wo.1, bf16[256,1024]{1,0:T(8,128)(2,1)} %wu.1, ...), custom_call_target="tpu_custom_call" | custom-call | tf_op jit(solution)/shard_map/evolve/pallas_call | solution.py:450
  65.8 1.7 %copy.14 = f32[1,2,1,128,256]{4,3,2,1,0:T(8,128)} copy(f32[1,2,1,128,256]{4,3,2,1,0:T(8,128)} %bitcast.8) | data formatting | bytes 524288
